TPU v7x, 32 devices: a whole 2x2x4 slice. The times are simulated.
32 devices in a mesh: kv: 2 (over y), blk: 16 (over z, x, core).
Axes of the slice: x: 2, y: 2, z: 4, core: 2. Of those that a mesh axis runs over, the one named last changes fastest.
Arguments:
- hidden_in: bfloat16 [8192, 1280], P('blk'), may hold values from -6 to 6
- w_query: bfloat16 [1280, 1280], P(None, 'kv'), may hold values from -0.15625 to 0.15625
- w_key: bfloat16 [1280, 1280], P(None, 'kv'), may hold values from -0.15625 to 0.15625
- w_value: bfloat16 [1280, 1280], P(None, 'kv'), may hold values from -0.15625 to 0.15625
- w_out: bfloat16 [1280, 1280], P('kv'), may hold values from -0.15625 to 0.15625
- head_gain: float32 [1280], P('kv'), may hold values from 1 to 2.5
- eigen_rate: float32 [1280], replicated, may hold values from 0.15 to 0.6
- pool_keys: bfloat16 [64, 256, 1280], P('blk', None, 'kv'), may hold values from -2 to 2
- pool_values: bfloat16 [64, 256, 1280], P('blk', None, 'kv'), may hold values from -6 to 6
- req_len: int32 [16], P('blk'), may hold values from 1 to 512, as said below
- prefix_len: int32 [16], P('blk'), may hold values from 0 to 4, as said below
- prefix_pages: int32 [16, 4], replicated, may hold values from 0 to 63, as said below
- placement: int32 [32], replicated, may hold values from 0 to 31, as said below
Outputs:
- layer_out: bfloat16 [8192, 1280], P('blk')
- new_keys: bfloat16 [32, 256, 1280], P('blk', None, 'kv')
- new_values: bfloat16 [32, 256, 1280], P('blk', None, 'kv')
Inputs may be any that keep to these rules, and one draw needn't show every extreme that they name: `req_len`: some request has all 512 tokens live. `prefix_len`: some request has 4 cached pages. Page prefix_pages[r, s] lies among pages h * 4 to (h + 1) * 4 - 1 with h = (r + 1 + s * 4) mod 16, for every slot s. Each page once; placement[b] lies among pages e * 2 to (e + 1) * 2 - 1 with e = (b // 2 + (2 * (b mod 2) + 1) * 4) mod 16.
All inputs are finite; a program needn't handle non-finite values.
Results may differ from a plain program's by a relative error of at most 0.0067.
Values may be sent and summed in bfloat16 or wider, within the bound.
No kernel may reach another device: no remote copies, remote signals or barrier semaphores. Data moves between devices by JAX's collectives and lax.ppermute only.
A program may use at most 128 MiB of HBM per device.

v0:
```python
import math

import jax
import jax.numpy as jnp
from jax import lax
from jax.sharding import PartitionSpec as P

HD = 64
PAGE = 256
PMAX = 4


epsilon = 1e-06


def from_behind(block, axis, distance):
    devices = range(lax.axis_size(axis))
    route = [((i - distance) % len(devices), i) for i in devices]
    return lax.ppermute(block, axis, route)


def rms_scale(values):
    return values * lax.rsqrt(jnp.mean(values * values, axis=-1, keepdims=True) + epsilon)


def head_normed(projected, head_gain):
    count = projected.shape[0]
    split_heads = projected.reshape(count, -1, HD)
    return (rms_scale(split_heads).reshape(count, -1) * head_gain).astype(jnp.bfloat16)


def attend(query_heads, key_rows, value_rows, visible):
    key_heads = key_rows.reshape(key_rows.shape[0], -1, HD)
    value_heads = value_rows.reshape(value_rows.shape[0], -1, HD)
    scores = jnp.einsum(
        "qhd,khd->hqk", query_heads, key_heads, preferred_element_type=jnp.float32
    ) / math.sqrt(HD)
    weights = jnp.where(visible, jnp.exp(scores), 0.0)
    totals = jnp.sum(weights, axis=-1)
    mixed = jnp.einsum(
        "hqk,khd->qhd",
        weights.astype(jnp.bfloat16),
        value_heads,
        preferred_element_type=jnp.float32,
    )
    return (totals, mixed)


def fetch_page(pool_keys, pool_values, prefix_pages, slot_index):
    devices = lax.axis_size("blk")
    here = lax.axis_index("blk")
    offset = slot_index * devices // PMAX + 1
    asker = (here - offset) % devices
    local = prefix_pages[asker, slot_index] % pool_keys.shape[0]
    send_keys = lax.dynamic_index_in_dim(pool_keys, local, 0, keepdims=False)
    send_values = lax.dynamic_index_in_dim(pool_values, local, 0, keepdims=False)
    return from_behind((send_keys, send_values), "blk", devices - offset)


def relay(key_rows, value_rows, placement):
    devices = lax.axis_size("blk")
    here = lax.axis_index("blk")
    blocks = key_rows.shape[0] // PAGE
    width = key_rows.shape[1]
    key_pages = key_rows.reshape(blocks, PAGE, width)
    value_pages = value_rows.reshape(blocks, PAGE, width)
    key_out = jnp.zeros_like(key_pages)
    value_out = jnp.zeros_like(value_pages)
    for block_index in range(blocks):
        offset = (2 * block_index + 1) * devices // (2 * blocks)
        key_recv, value_recv = from_behind(
            (key_pages[block_index], value_pages[block_index]), "blk", offset
        )
        source = (here - offset) % devices
        target = placement[source * blocks + block_index] % blocks
        key_out = lax.dynamic_update_index_in_dim(key_out, key_recv, target, 0)
        value_out = lax.dynamic_update_index_in_dim(value_out, value_recv, target, 0)
    return (key_out, value_out)


def body(
    hidden_in,
    w_query,
    w_key,
    w_value,
    w_out,
    head_gain,
    eigen_rate,
    pool_keys,
    pool_values,
    req_len,
    prefix_len,
    prefix_pages,
    placement,
):
    tokens_here = hidden_in.shape[0]
    width_half = w_query.shape[1]
    heads_here = width_half // HD
    hidden_f = hidden_in.astype(jnp.float32)
    row_scale = lax.rsqrt(jnp.mean(hidden_f * hidden_f, axis=-1, keepdims=True) + epsilon)
    anchor = hidden_f * row_scale
    queries = head_normed(
        jnp.dot(hidden_in, w_query, preferred_element_type=jnp.float32), head_gain
    )
    key_rows = head_normed(jnp.dot(hidden_in, w_key, preferred_element_type=jnp.float32), head_gain)
    value_rows = (
        jnp.dot(hidden_in, w_value, preferred_element_type=jnp.float32) * row_scale
    ).astype(jnp.bfloat16)
    live_count = req_len[0]
    depth = prefix_len[0]
    query_heads = queries.reshape(tokens_here, heads_here, HD)
    row_index = jnp.arange(tokens_here, dtype=jnp.int32)[:, None]
    col_index = jnp.arange(tokens_here, dtype=jnp.int32)[None, :]
    own_visible = ((col_index <= row_index) & (col_index < live_count))[None]
    totals, mixed = attend(query_heads, key_rows, value_rows, own_visible)
    fetched_keys = []
    fetched_values = []
    for slot_index in range(PMAX):
        page_keys, page_values = fetch_page(pool_keys, pool_values, prefix_pages, slot_index)
        fetched_keys.append(page_keys)
        fetched_values.append(page_values)
    cached_keys = jnp.concatenate(fetched_keys, axis=0)
    cached_values = jnp.concatenate(fetched_values, axis=0)
    page_number = jnp.arange(cached_keys.shape[0], dtype=jnp.int32) // PAGE
    cached_visible = (page_number < depth)[None, None, :]
    more_totals, more_mixed = attend(query_heads, cached_keys, cached_values, cached_visible)
    totals = totals + more_totals
    mixed = mixed + more_mixed
    attended = (mixed / totals.T[:, :, None]).astype(jnp.bfloat16).reshape(tokens_here, width_half)
    partial_branch = jnp.dot(attended, w_out, preferred_element_type=jnp.float32)
    branch = lax.psum(partial_branch, "kv")
    updated = anchor + eigen_rate * (rms_scale(branch) - anchor)
    layer_out = rms_scale(updated).astype(jnp.bfloat16)
    new_keys, new_values = relay(key_rows, value_rows, placement)
    return (layer_out, new_keys, new_values)


def solution(mesh):
    in_specs = (
        P("blk", None),
        P(None, "kv"),
        P(None, "kv"),
        P(None, "kv"),
        P("kv", None),
        P("kv"),
        P(),
        P("blk", None, "kv"),
        P("blk", None, "kv"),
        P("blk"),
        P("blk"),
        P(),
        P(),
    )
    out_specs = (P("blk", None), P("blk", None, "kv"), P("blk", None, "kv"))
    return jax.shard_map(body, mesh=mesh, in_specs=in_specs, out_specs=out_specs, check_vma=False)
```

profile of v0, /device:TPU:16, one launch (start us, length us, event | category | flops | bytes accessed | tf_op | source)
XLA Modules:
  0.0 200.7 jit_solution(12353417326446892025)
XLA Ops:
  16.5 2.5 %dynamic-slice_bitcast_fusion.3 = (bf16[256,640]{1,0:T(8,128)(2,1)}, bf16[256,640]{1,0:T(8,128)(2,1)}, bf16[256,640]{1,0:T(8,128)(2,1)}, bf16[256,640]{1,0:T(8,128)(2,1)}) fusion(bf16[4,256,640]{2,1,0:T(8,128)(2,1)} %param.20, s32[]{:T(128)S(6)} %select_n.116, s32[]{:T(128)S(6)} %select_n.120, s32[]{:T(128)S(6)} %select_n.128, s32[]{:T(128)S(6)} %select_n.124), kind=kLoop, calls=%fused_computation.39 | loop fusion | bytes 2621456 | tf_op jit(solution)/shard_map/jit(dynamic_index_in_dim)/squeeze | solution.py:55
  20.7 4.4 %collective-permute-start.6 = (bf16[256,640]{1,0:T(8,128)(2,1)}, bf16[256,640]{1,0:T(8,128)(2,1)}, u32[]{:S(2)}, u32[]{:S(2)}) collective-permute-start(bf16[256,640]{1,0:T(8,128)(2,1)} %get-tuple-element.6), channel_id=1, source_target_pairs={{9,0},{10,1},{11,2},{12,3},{13,4},{14,5},{15,6},{0,7},{1,8},{2,9},... | collective-permute-start | bytes 983048 | tf_op jit(solution)/shard_map/ppermute | solution.py:19
  29.3 2.0 %fusion.22 = bf16[512,640]{1,0:T(8,128)(2,1)} fusion(bf16[512,1280]{1,0:T(8,128)(2,1)S(1)} %copy-done.3, bf16[1280,640]{1,0:T(8,128)(2,1)S(1)} %copy-done.17, f32[512]{0:T(512)S(1)} %add_rsqrt_fusion.4), kind=kOutput, calls=%fused_computation.24 | convolution fusion | flops 839516160 | bytes 3606528 | tf_op jit(solution)/shard_map/dot_general | solution.py:107
  31.3 2.2 %copy.21 = bf16[512,640]{0,1:T(8,128)(2,1)} copy(bf16[512,640]{1,0:T(8,128)(2,1)} %fusion.22) | data formatting | bytes 1310720 | tf_op jit(solution)/shard_map/convert_element_type | solution.py:108
  33.5 2.7 %fusion.38 = (f32[512,640]{1,0:T(8,128)}, f32[512,640]{1,0:T(8,128)}) fusion(bf16[512,1280]{1,0:T(8,128)(2,1)S(1)} %copy-done.3, bf16[1280,640]{1,0:T(8,128)(2,1)S(1)} %copy-done), kind=kOutput, calls=%fused_computation.71 | convolution fusion | flops 839188480 | bytes 5570560 | tf_op jit(solution)/shard_map/dot_general | solution.py:103
  39.7 4.1 %fusion.37 = (f32[512,640]{1,0:T(8,128)}, f32[512,640]{1,0:T(8,128)}) fusion(bf16[512,1280]{1,0:T(8,128)(2,1)S(1)} %copy-done.3, bf16[1280,640]{1,0:T(8,128)(2,1)} %param.15), kind=kOutput, calls=%fused_computation.70 | convolution fusion | flops 839188480 | bytes 5570560 | tf_op jit(solution)/shard_map/dot_general | solution.py:105
  47.4 2.8 %multiply_convert_fusion.1 = (bf16[512,640]{1,0:T(8,128)(2,1)S(1)}, bf16[512,640]{1,0:T(8,128)(2,1)S(1)}) fusion(f32[512,640]{1,0:T(8,128)} %get-tuple-element.24, f32[512,640]{1,0:T(8,128)} %copy.26, f32[640]{0:T(1024)S(1)} %copy-done.15, f32[512,640]{1,0:T(8,128)} %get-tuple-element.26, f32[512,640]{1,0:T(8,128)} %copy.23), kind=kLoop, calls=%fused_computation.28 | loop fusion | flops 1966080 | bytes 6556160 | tf_op jit(solution)/shard_map/convert_element_type | solution.py:29
  52.4 4.7 %fusion.5 = (f32[10,512]{1,0:T(8,128)}, f32[10,512,512]{1,2,0:T(8,128)S(1)}) fusion(pred[512,512]{0,1:T(8,128)(4,1)S(1)} %fusion.23, bf16[512,10,64]{0,2,1:T(8,128)(2,1)} %bitcast.71, bf16[512,10,64]{0,2,1:T(8,128)(2,1)} %bitcast.73), kind=kOutput, calls=%fused_computation.6 | convolution fusion | flops 343403520 | bytes 12079104 | tf_op jit(solution)/shard_map/qhd,khd->hqk/dot_general | solution.py:35
  57.2 2.5 %collective-permute-start.2 = (bf16[256,640]{1,0:T(8,128)(2,1)S(1)}, bf16[256,640]{1,0:T(8,128)(2,1)}, u32[]{:S(2)}, u32[]{:S(2)}) collective-permute-start(bf16[256,640]{1,0:T(8,128)(2,1)S(1)} %copy-done.12), channel_id=1, source_target_pairs={{9,0},{10,1},{11,2},{12,3},{13,4},{14,5},{15,6},{0,7},{1,8},{2,9},... | collective-permute-start | bytes 983048 | tf_op jit(solution)/shard_map/ppermute | solution.py:19
  59.7 2.9 %fusion.7 = f32[10,64,512]{2,1,0:T(8,128)} fusion(bf16[512,10,64]{0,2,1:T(8,128)(2,1)S(1)} %bitcast.68, f32[10,512,512]{1,2,0:T(8,128)S(1)} %get-tuple-element.28, pred[512,512]{0,1:T(8,128)(4,1)S(1)} %fusion.23), kind=kOutput, calls=%fused_computation.8 | convolution fusion | flops 343408640 | bytes 12713984 | tf_op jit(solution)/shard_map/hqk,khd->qhd/dot_general | solution.py:40
  63.3 2.4 %pad_maximum_fusion.1 = bf16[1024,640]{1,0:T(8,128)(2,1)} fusion(bf16[256,640]{1,0:T(8,128)(2,1)} %collective-permute-done.7, bf16[256,640]{1,0:T(8,128)(2,1)} %collective-permute-done.6, bf16[256,640]{1,0:T(8,128)(2,1)} %collective-permute-done.5, bf16[256,640]{1,0:T(8,128)(2,1)S(1)} %collective-permute-done.4), kind=kLoop, calls=%fused_computation.26 | loop fusion | flops 5242880 | bytes 2621440 | tf_op jit(solution)/shard_map/concatenate | solution.py:122
  65.7 2.5 %copy.30 = bf16[1024,640]{0,1:T(8,128)(2,1)} copy(bf16[1024,640]{1,0:T(8,128)(2,1)} %pad_maximum_fusion.1) | data formatting | bytes 2621440 | tf_op jit(solution)/shard_map/concatenate | solution.py:122
  68.2 11.4 %collective-permute-done.1 = bf16[256,640]{1,0:T(8,128)(2,1)} collective-permute-done((bf16[256,640]{1,0:T(8,128)(2,1)}, bf16[256,640]{1,0:T(8,128)(2,1)}, u32[]{:S(2)}, u32[]{:S(2)}) %collective-permute-start.1) | collective-permute-done | bytes 327712 | tf_op jit(solution)/shard_map/ppermute | solution.py:19
  79.6 2.5 %pad_maximum_fusion = bf16[1024,640]{1,0:T(8,128)(2,1)} fusion(bf16[256,640]{1,0:T(8,128)(2,1)} %collective-permute-done.3, bf16[256,640]{1,0:T(8,128)(2,1)} %collective-permute-done.2, bf16[256,640]{1,0:T(8,128)(2,1)} %collective-permute-done.1, bf16[256,640]{1,0:T(8,128)(2,1)} %collective-permute-done), kind=kLoop, calls=%fused_computation.25 | loop fusion | flops 5242880 | bytes 2621440 | tf_op jit(solution)/shard_map/concatenate | solution.py:123
  82.1 2.6 %copy.29 = bf16[1024,640]{0,1:T(8,128)(2,1)} copy(bf16[1024,640]{1,0:T(8,128)(2,1)} %pad_maximum_fusion) | data formatting | bytes 2621440 | tf_op jit(solution)/shard_map/concatenate | solution.py:123
  84.7 10.9 %fusion = (f32[10,512]{1,0:T(8,128)S(1)}, f32[10,512,1024]{2,1,0:T(8,128)}) fusion(pred[1024]{0:T(1024)(128)(4,1)S(1)} %fusion.26, bf16[512,10,64]{0,2,1:T(8,128)(2,1)S(1)} %bitcast.72, bf16[1024,10,64]{0,2,1:T(8,128)(2,1)} %bitcast.69), kind=kOutput, calls=%fused_computation.1 | convolution fusion | flops 686812160 | bytes 22959104 | tf_op jit(solution)/shard_map/qhd,khd->hqk/dot_general | solution.py:35
  95.6 9.0 %divide_convert_fusion = bf16[512,10,64]{0,2,1:T(8,128)(2,1)S(1)} fusion(f32[10,64,512]{2,1,0:T(8,128)S(1)} %copy-done.6, bf16[1024,10,64]{0,2,1:T(8,128)(2,1)S(1)} %bitcast.70, f32[10,512,1024]{2,1,0:T(8,128)} %get-tuple-element.30, pred[1024]{0:T(1024)(128)(4,1)S(1)} %fusion.26, f32[512,10]{0,1:T(8,128)S(1)} %add_bitcast_fusion), kind=kOutput, calls=%fused_computation.27 | convolution fusion | flops 687800320 | bytes 24269824 | tf_op jit(solution)/shard_map/hqk,khd->qhd/dot_general | solution.py:40
  104.7 2.7 %fusion.39 = f32[512,1280]{1,0:T(8,128)} fusion(bf16[512,640]{0,1:T(8,128)(2,1)S(1)} %bitcast.74, bf16[640,1280]{1,0:T(8,128)(2,1)S(1)} %copy-done.18), kind=kOutput, calls=%fused_computation.72 | convolution fusion | flops 838860800 | bytes 4915200 | tf_op jit(solution)/shard_map/dot_general | solution.py:130
  109.3 5.9 %collective-permute-start.10 = (bf16[256,640]{1,0:T(8,128)(2,1)}, bf16[256,640]{1,0:T(8,128)(2,1)}, u32[]{:S(2)}, u32[]{:S(2)}) collective-permute-start(bf16[256,640]{1,0:T(8,128)(2,1)} %get-tuple-element.12), channel_id=1, source_target_pairs={{12,0},{13,1},{14,2},{15,3},{0,4},{1,5},{2,6},{3,7},{4,8},{5,9},{6... | collective-permute-start | bytes 983048 | tf_op jit(solution)/shard_map/ppermute | solution.py:19
  123.7 6.4 %collective-permute-done.8 = bf16[256,640]{1,0:T(8,128)(2,1)} collective-permute-done((bf16[256,640]{1,0:T(8,128)(2,1)}, bf16[256,640]{1,0:T(8,128)(2,1)}, u32[]{:S(2)}, u32[]{:S(2)}) %collective-permute-start.8) | collective-permute-done | bytes 327712 | tf_op jit(solution)/shard_map/ppermute | solution.py:19
  131.2 6.1 %collective-permute-done.11 = bf16[256,640]{1,0:T(8,128)(2,1)} collective-permute-done((bf16[256,640]{1,0:T(8,128)(2,1)S(1)}, bf16[256,640]{1,0:T(8,128)(2,1)}, u32[]{:S(2)}, u32[]{:S(2)}) %collective-permute-start.11) | collective-permute-done | bytes 327712 | tf_op jit(solution)/shard_map/ppermute | solution.py:19
  138.4 6.0 %collective-permute-done.9 = bf16[256,640]{1,0:T(8,128)(2,1)} collective-permute-done((bf16[256,640]{1,0:T(8,128)(2,1)S(1)}, bf16[256,640]{1,0:T(8,128)(2,1)}, u32[]{:S(2)}, u32[]{:S(2)}) %collective-permute-start.9) | collective-permute-done | bytes 327712 | tf_op jit(solution)/shard_map/ppermute | solution.py:19
  146.2 42.5 %all-reduce.2.cloned.1.call-done = f32[512,1280]{1,0:T(8,128)} async-done(((f32[512,1280]{1,0:T(8,128)}), f32[512,1280]{1,0:T(8,128)}) %all-reduce.2.cloned.1.call-update) | async-done | bytes 2621456 | tf_op jit(solution)/shard_map/psum | solution.py:131
  188.7 2.1 %multiply_reduce_fusion.1 = f32[512]{0:T(512)S(1)} fusion(f32[512,1280]{1,0:T(8,128)} %all-reduce.2.cloned.1.call-done), kind=kLoop, calls=%fused_computation.20 | loop fusion | flops 1310208 | bytes 2623488 | tf_op jit(solution)/shard_map/reduce_sum | solution.py:23
  (90 shorter events, 29.5 us)
Async XLA Ops:
  7.2 26.3 %copy-start = (bf16[1280,640]{1,0:T(8,128)(2,1)S(1)}, bf16[1280,640]{1,0:T(8,128)(2,1)}, u32[]{:S(2)}) copy-start(bf16[1280,640]{1,0:T(8,128)(2,1)} %param.14) | copy-start | bytes 4915204
  7.2 181.5 %all-reduce.2.cloned.1.call-start = ((), (), s32[]{:S(2)}) async-start(), calls=%async_computation | async-start | bytes 5242880 | tf_op jit(solution)/shard_map/psum | solution.py:131
  16.5 8.6 %copy-start.8 = (bf16[4,256,640]{2,1,0:T(8,128)(2,1)S(1)}, bf16[4,256,640]{2,1,0:T(8,128)(2,1)}, u32[]{:S(2)}) copy-start(bf16[4,256,640]{2,1,0:T(8,128)(2,1)} %param.21) | copy-start | bytes 3932164
  19.0 9.8 %copy-start.3 = (bf16[512,1280]{1,0:T(8,128)(2,1)S(1)}, bf16[512,1280]{1,0:T(8,128)(2,1)}, u32[]{:S(2)}) copy-start(bf16[512,1280]{1,0:T(8,128)(2,1)} %param.13) | copy-start | bytes 3932164
  19.0 38.0 %collective-permute-start.4 = (bf16[256,640]{1,0:T(8,128)(2,1)}, bf16[256,640]{1,0:T(8,128)(2,1)S(1)}, u32[]{:S(2)}, u32[]{:S(2)}) collective-permute-start(bf16[256,640]{1,0:T(8,128)(2,1)} %get-tuple-element.3), channel_id=1, source_target_pairs={{1,0},{2,1},{3,2},{4,3},{5,4},{6,5},{7,6},{8,7},{9,8},{10,9},{11,1... | collective-permute-start | bytes 983048 | tf_op jit(solution)/shard_map/ppermute | solution.py:19
  19.8 37.2 %collective-permute-start.5 = (bf16[256,640]{1,0:T(8,128)(2,1)}, bf16[256,640]{1,0:T(8,128)(2,1)}, u32[]{:S(2)}, u32[]{:S(2)}) collective-permute-start(bf16[256,640]{1,0:T(8,128)(2,1)} %get-tuple-element.4), channel_id=1, source_target_pairs={{5,0},{6,1},{7,2},{8,3},{9,4},{10,5},{11,6},{12,7},{13,8},{14,9},{... | collective-permute-start | bytes 983048 | tf_op jit(solution)/shard_map/ppermute | solution.py:19
  20.4 36.8 %collective-permute-start.7 = (bf16[256,640]{1,0:T(8,128)(2,1)}, bf16[256,640]{1,0:T(8,128)(2,1)}, u32[]{:S(2)}, u32[]{:S(2)}) collective-permute-start(bf16[256,640]{1,0:T(8,128)(2,1)} %get-tuple-element.5), channel_id=1, source_target_pairs={{13,0},{14,1},{15,2},{0,3},{1,4},{2,5},{3,6},{4,7},{5,8},{6,9},{7,... | collective-permute-start | bytes 983048 | tf_op jit(solution)/shard_map/ppermute | solution.py:19
  20.7 8.6 %copy-start.17 = (bf16[1280,640]{1,0:T(8,128)(2,1)S(1)}, bf16[1280,640]{1,0:T(8,128)(2,1)}, u32[]{:S(2)}) copy-start(bf16[1280,640]{1,0:T(8,128)(2,1)} %param.16) | copy-start | bytes 4915204
  20.7 42.6 %collective-permute-start.6 = (bf16[256,640]{1,0:T(8,128)(2,1)}, bf16[256,640]{1,0:T(8,128)(2,1)}, u32[]{:S(2)}, u32[]{:S(2)}) collective-permute-start(bf16[256,640]{1,0:T(8,128)(2,1)} %get-tuple-element.6), channel_id=1, source_target_pairs={{9,0},{10,1},{11,2},{12,3},{13,4},{14,5},{15,6},{0,7},{1,8},{2,9},... | collective-permute-start | bytes 983048 | tf_op jit(solution)/shard_map/ppermute | solution.py:19
  26.3 41.9 %collective-permute-start = (bf16[256,640]{1,0:T(8,128)(2,1)}, bf16[256,640]{1,0:T(8,128)(2,1)}, u32[]{:S(2)}, u32[]{:S(2)}) collective-permute-start(bf16[256,640]{1,0:T(8,128)(2,1)} %get-tuple-element.7), channel_id=1, source_target_pairs={{1,0},{2,1},{3,2},{4,3},{5,4},{6,5},{7,6},{8,7},{9,8},{10,9},{11,1... | collective-permute-start | bytes 983048 | tf_op jit(solution)/shard_map/ppermute | solution.py:19
  57.1 22.5 %collective-permute-start.1 = (bf16[256,640]{1,0:T(8,128)(2,1)}, bf16[256,640]{1,0:T(8,128)(2,1)}, u32[]{:S(2)}, u32[]{:S(2)}) collective-permute-start(bf16[256,640]{1,0:T(8,128)(2,1)} %get-tuple-element.8), channel_id=1, source_target_pairs={{5,0},{6,1},{7,2},{8,3},{9,4},{10,5},{11,6},{12,7},{13,8},{14,9},{... | collective-permute-start | bytes 983048 | tf_op jit(solution)/shard_map/ppermute | solution.py:19
  57.1 22.5 %collective-permute-start.3 = (bf16[256,640]{1,0:T(8,128)(2,1)}, bf16[256,640]{1,0:T(8,128)(2,1)}, u32[]{:S(2)}, u32[]{:S(2)}) collective-permute-start(bf16[256,640]{1,0:T(8,128)(2,1)} %get-tuple-element.9), channel_id=1, source_target_pairs={{13,0},{14,1},{15,2},{0,3},{1,4},{2,5},{3,6},{4,7},{5,8},{6,9},{7,... | collective-permute-start | bytes 983048 | tf_op jit(solution)/shard_map/ppermute | solution.py:19
  57.2 22.4 %collective-permute-start.2 = (bf16[256,640]{1,0:T(8,128)(2,1)S(1)}, bf16[256,640]{1,0:T(8,128)(2,1)}, u32[]{:S(2)}, u32[]{:S(2)}) collective-permute-start(bf16[256,640]{1,0:T(8,128)(2,1)S(1)} %copy-done.12), channel_id=1, source_target_pairs={{9,0},{10,1},{11,2},{12,3},{13,4},{14,5},{15,6},{0,7},{1,8},{2,9},... | collective-permute-start | bytes 983048 | tf_op jit(solution)/shard_map/ppermute | solution.py:19
  84.6 10.9 %copy-start.14 = (f32[10,512]{1,0:T(8,128)S(1)}, f32[10,512]{1,0:T(8,128)}, u32[]{:S(2)}) copy-start(f32[10,512]{1,0:T(8,128)} %get-tuple-element.27) | copy-start | bytes 61444
  84.7 11.0 %copy-start.6 = (f32[10,64,512]{2,1,0:T(8,128)S(1)}, f32[10,64,512]{2,1,0:T(8,128)}, u32[]{:S(2)}) copy-start(f32[10,64,512]{2,1,0:T(8,128)} %fusion.7) | copy-start | bytes 3932164
  84.7 11.0 %copy-start.7 = (bf16[1024,640]{0,1:T(8,128)(2,1)S(1)}, bf16[1024,640]{0,1:T(8,128)(2,1)}, u32[]{:S(2)}) copy-start(bf16[1024,640]{0,1:T(8,128)(2,1)} %copy.29) | copy-start | bytes 3932164
  95.6 9.0 %copy-start.18 = (bf16[640,1280]{1,0:T(8,128)(2,1)S(1)}, bf16[640,1280]{1,0:T(8,128)(2,1)}, u32[]{:S(2)}) copy-start(bf16[640,1280]{1,0:T(8,128)(2,1)} %param.17) | copy-start | bytes 4915204
  108.5 9.5 %copy-start.16 = (s32[32]{0:T(128)S(1)}, s32[32]{0:T(128)}, u32[]{:S(2)}) copy-start(s32[32]{0:T(128)} %param.25) | copy-start | bytes 388
  109.3 13.4 %collective-permute-start.10 = (bf16[256,640]{1,0:T(8,128)(2,1)}, bf16[256,640]{1,0:T(8,128)(2,1)}, u32[]{:S(2)}, u32[]{:S(2)}) collective-permute-start(bf16[256,640]{1,0:T(8,128)(2,1)} %get-tuple-element.12), channel_id=1, source_target_pairs={{12,0},{13,1},{14,2},{15,3},{0,4},{1,5},{2,6},{3,7},{4,8},{5,9},{6... | collective-permute-start | bytes 983048 | tf_op jit(solution)/shard_map/ppermute | solution.py:19
  115.9 14.2 %collective-permute-start.8 = (bf16[256,640]{1,0:T(8,128)(2,1)}, bf16[256,640]{1,0:T(8,128)(2,1)}, u32[]{:S(2)}, u32[]{:S(2)}) collective-permute-start(bf16[256,640]{1,0:T(8,128)(2,1)} %get-tuple-element.14), channel_id=1, source_target_pairs={{12,0},{13,1},{14,2},{15,3},{0,4},{1,5},{2,6},{3,7},{4,8},{5,9},{6... | collective-permute-start | bytes 983048 | tf_op jit(solution)/shard_map/ppermute | solution.py:19
  116.4 20.9 %collective-permute-start.11 = (bf16[256,640]{1,0:T(8,128)(2,1)S(1)}, bf16[256,640]{1,0:T(8,128)(2,1)}, u32[]{:S(2)}, u32[]{:S(2)}) collective-permute-start(bf16[256,640]{1,0:T(8,128)(2,1)S(1)} %get-tuple-element.11), channel_id=1, source_target_pairs={{4,0},{5,1},{6,2},{7,3},{8,4},{9,5},{10,6},{11,7},{12,8},{13,9},{1... | collective-permute-start | bytes 983048 | tf_op jit(solution)/shard_map/ppermute | solution.py:19
  117.9 26.4 %collective-permute-start.9 = (bf16[256,640]{1,0:T(8,128)(2,1)S(1)}, bf16[256,640]{1,0:T(8,128)(2,1)}, u32[]{:S(2)}, u32[]{:S(2)}) collective-permute-start(bf16[256,640]{1,0:T(8,128)(2,1)S(1)} %get-tuple-element.13), channel_id=1, source_target_pairs={{4,0},{5,1},{6,2},{7,3},{8,4},{9,5},{10,6},{11,7},{12,8},{13,9},{1... | collective-permute-start | bytes 983048 | tf_op jit(solution)/shard_map/ppermute | solution.py:19
  138.3 52.5 %copy-start.11 = (bf16[2,256,640]{2,1,0:T(8,128)(2,1)}, bf16[2,256,640]{2,1,0:T(8,128)(2,1)S(1)}, u32[]{:S(2)}) copy-start(bf16[2,256,640]{2,1,0:T(8,128)(2,1)S(1)} %bitcast_dynamic-update-slice_fusion) | copy-start | bytes 1966084
  138.4 52.5 %copy-start.13 = (f32[1280]{0:T(1024)S(1)}, f32[1280]{0:T(1024)}, u32[]{:S(2)}) copy-start(f32[1280]{0:T(1024)} %param.19) | copy-start | bytes 15364
  (8 other events, 22.5 us)
Sparse Core Ops, SparseCore 0:
  107.5 81.1 all-reduce.1
where the time goes:
time: 203 us; the launch traced here: 201 us
  waiting for transfers between devices  72.4 us (36%)
  matrix products  39.1 us (19%)
  local copies, waits for them, and re-layouts  29.9 us (15%)
  between operations  27.5 us (14%)
  starting transfers between devices  18.6 us (9%)
  other arithmetic  13.2 us (7%)
    psum x1, waiting for transfers between devices, body(): branch = lax.psum(partial_branch, 'kv')  42.5 us
    ppermute x12, waiting for transfers between devices, from_behind(): return lax.ppermute(block, axis, route)  29.9 us
    ppermute x12, starting transfers between devices, from_behind(): return lax.ppermute(block, axis, route)  18.6 us
    dot_general x2, matrix products, attend(): jnp.einsum('qhd,khd->hqk', query_heads, key_heads, preferred_element_type...  15.6 us
    dot_general x2, matrix products, attend(): jnp.einsum('hqk,khd->qhd', weights.astype(jnp.bfloat16), value_heads, pre...  11.9 us
    dot_general x1, matrix products, body(): jnp.dot(hidden_in, w_key, preferred_element_type=jnp.float32)  4.1 us
  transfers between devices with their start and end apart: 13, of which 5 were waited for; matrix products, arithmetic and copies ran while one was open for 22% of the time, Pallas kernels for 0%

commit v1 on v0

v1 whole, which is shorter than its diff:
```python
import functools
import math

import jax
import jax.numpy as jnp
from jax import lax
from jax.experimental import pallas as pl
from jax.experimental.pallas import tpu as pltpu
from jax.sharding import PartitionSpec as P

HD = 64
PAGE = 256
PMAX = 4
LANES = 128
GROUPS = (256, 256, 128)
VMEM_LIMIT = 48 * 1024 * 1024

epsilon = 1e-06

f32 = jnp.float32
bf16 = jnp.bfloat16


def from_behind(block, axis, distance):
    devices = range(lax.axis_size(axis))
    route = [((i - distance) % len(devices), i) for i in devices]
    return lax.ppermute(block, axis, route)


def group_slices(width):
    slices, start = [], 0
    for size in GROUPS:
        slices.append((start, size))
        start += size
    assert start == width
    return slices


def params():
    return pltpu.CompilerParams(vmem_limit_bytes=VMEM_LIMIT)


def cost(flops, bytes_accessed, transcendentals=0):
    return pl.CostEstimate(
        flops=flops, bytes_accessed=bytes_accessed, transcendentals=transcendentals
    )


def pack_kernel(slices, blocks, local_ref, kv_ref, hidden, keys, values, *rest):
    outs, sem = rest[:-1], rest[-1]
    half = PAGE // 2
    copies = []
    for block in range(blocks):
        rows = pl.ds(pl.multiple_of(block * PAGE + kv_ref[0] * half, half), half)
        copies.append((hidden.at[rows], outs[block]))
    place = blocks
    for start, size in slices:
        for slot in range(PMAX):
            local = local_ref[slot]
            columns = pl.ds(start, size)
            copies.append((keys.at[local, :, columns], outs[place].at[0]))
            copies.append((values.at[local, :, columns], outs[place].at[1]))
            place += 1
    started = []
    for index, (source, target) in enumerate(copies):
        copy = pltpu.make_async_copy(source, target, sem.at[index])
        copy.start()
        started.append(copy)
    for copy in started:
        copy.wait()


def pack(hidden_in, pool_keys, pool_values, local, kv_index, blocks):
    width = pool_keys.shape[2]
    slices = group_slices(width)
    outs = [jax.ShapeDtypeStruct((PAGE // 2, hidden_in.shape[1]), bf16)] * blocks
    for _, size in slices:
        outs += [jax.ShapeDtypeStruct((2, PAGE, size), bf16)] * PMAX
    count = blocks + 2 * PMAX * len(slices)
    result = pl.pallas_call(
        functools.partial(pack_kernel, slices, blocks),
        grid_spec=pltpu.PrefetchScalarGridSpec(
            num_scalar_prefetch=2,
            grid=(1,),
            in_specs=[pl.BlockSpec(memory_space=pl.ANY)] * 3,
            out_specs=[pl.BlockSpec(memory_space=pl.ANY)] * len(outs),
            scratch_shapes=[pltpu.SemaphoreType.DMA((count,))],
        ),
        out_shape=outs,
        compiler_params=params(),
        name="pack",
    )(local, kv_index, hidden_in, pool_keys, pool_values)
    relays = result[:blocks]
    pages = [result[blocks + PMAX * g : blocks + PMAX * (g + 1)] for g in range(len(slices))]
    return relays, pages


def head_sum_matrix():
    rows = lax.broadcasted_iota(jnp.int32, (LANES, LANES), 0) // HD
    cols = lax.broadcasted_iota(jnp.int32, (LANES, LANES), 1) // HD
    return jnp.where(rows == cols, 1.0 / HD, 0.0).astype(bf16)


def head_norm(projected, gain, matrix):
    parts = []
    for start in range(0, projected.shape[1], LANES):
        part = projected[:, start : start + LANES]
        squares = part * part
        high = squares.astype(bf16)
        low = (squares - high.astype(f32)).astype(bf16)
        mean = jnp.dot(high, matrix, preferred_element_type=f32)
        mean += jnp.dot(low, matrix, preferred_element_type=f32)
        parts.append(part * lax.rsqrt(mean + epsilon) * gain[:, start : start + LANES])
    return jnp.concatenate(parts, axis=1) if len(parts) > 1 else parts[0]


def row_scale_of(hidden):
    hidden_f = hidden.astype(f32)
    return lax.rsqrt(jnp.mean(hidden_f * hidden_f, axis=-1, keepdims=True) + epsilon)


def project_kernel(slices, hidden, wq, wk, wv, gain, *outs):
    matrix = head_sum_matrix()
    rows_all = hidden.shape[0]
    for low in range(0, rows_all, PAGE):
        rows = slice(low, low + PAGE)
        x = hidden[rows, :]
        scale = row_scale_of(x)
        for g, (start, size) in enumerate(slices):
            cols = slice(start, start + size)
            q = jnp.dot(x, wq[:, cols], preferred_element_type=f32)
            q = head_norm(q, gain[:, cols], matrix).astype(bf16)
            outs[3 * g][rows, :] = q * jnp.asarray(1.0 / math.sqrt(HD), bf16)
            k = jnp.dot(x, wk[:, cols], preferred_element_type=f32)
            outs[3 * g + 1][rows, :] = head_norm(k, gain[:, cols], matrix).astype(bf16)
            v = jnp.dot(x, wv[:, cols], preferred_element_type=f32)
            outs[3 * g + 2][rows, :] = (v * scale).astype(bf16)


def project(hidden_in, wq, wk, wv, gain):
    tokens, depth = hidden_in.shape
    width = wq.shape[1]
    slices = group_slices(width)
    outs = []
    for _, size in slices:
        outs += [jax.ShapeDtypeStruct((tokens, size), bf16)] * 3
    flat = pl.pallas_call(
        functools.partial(project_kernel, slices),
        out_shape=outs,
        compiler_params=params(),
        cost_estimate=cost(6 * tokens * depth * width, 8 * 1024 * 1024),
        name="project",
    )(hidden_in, wq, wk, wv, gain)
    return [flat[3 * g : 3 * g + 3] for g in range(len(slices))]


def relay_kernel(slices, blocks, kv_ref, slot_ref, *refs):
    mine = refs[:blocks]
    theirs = refs[blocks : 2 * blocks]
    wk, wv, gain, key_out, value_out, rows_buf = refs[2 * blocks :]
    matrix = head_sum_matrix()
    half = PAGE // 2
    for block in range(blocks):
        near = pl.multiple_of(kv_ref[0] * half, half)
        far = pl.multiple_of((1 - kv_ref[0]) * half, half)
        rows_buf[pl.ds(near, half), :] = mine[block][...]
        rows_buf[pl.ds(far, half), :] = theirs[block][...]
        x = rows_buf[...]
        scale = row_scale_of(x)
        slot = slot_ref[block]
        for start, size in slices:
            cols = slice(start, start + size)
            k = jnp.dot(x, wk[:, cols], preferred_element_type=f32)
            key_out[slot, :, cols] = head_norm(k, gain[:, cols], matrix).astype(bf16)
            v = jnp.dot(x, wv[:, cols], preferred_element_type=f32)
            value_out[slot, :, cols] = (v * scale).astype(bf16)


def relay_project(mine, theirs, wk, wv, gain, kv_index, slots):
    blocks = len(mine)
    depth, width = wk.shape
    out = jax.ShapeDtypeStruct((blocks, PAGE, width), bf16)
    smem = pl.BlockSpec(memory_space=pltpu.SMEM)
    vmem = pl.BlockSpec(memory_space=pltpu.VMEM)
    return pl.pallas_call(
        functools.partial(relay_kernel, group_slices(width), blocks),
        in_specs=[smem, smem] + [vmem] * (2 * blocks + 3),
        out_specs=[vmem, vmem],
        out_shape=[out, out],
        scratch_shapes=[pltpu.VMEM((PAGE, depth), bf16)],
        compiler_params=params(),
        cost_estimate=cost(4 * blocks * PAGE * depth * width, 8 * 1024 * 1024),
        name="relay_project",
    )(kv_index, slots, *mine, *theirs, wk, wv, gain)


def attend_kernel(live_ref, depth_ref, q_ref, k_ref, v_ref, p0, p1, p2, p3, out):
    pages = (p0, p1, p2, p3)
    tokens, width = q_ref.shape
    live, depth = live_ref[0], depth_ref[0]
    lane = lax.broadcasted_iota(jnp.int32, (1, LANES), 1)
    row = lax.broadcasted_iota(jnp.int32, (PAGE, PAGE), 0)
    col = lax.broadcasted_iota(jnp.int32, (PAGE, PAGE), 1)
    causal = col <= row
    key_row = lax.broadcasted_iota(jnp.int32, (PAGE, LANES), 0)
    blocks = tokens // PAGE
    for start in range(0, width, LANES):
        cols = slice(start, start + LANES)
        keys, values = [], []
        for b in range(blocks):
            rows = slice(b * PAGE, (b + 1) * PAGE)
            keep = (key_row + b * PAGE) < live
            keys.append(k_ref[rows, cols])
            shown = jnp.where(keep, v_ref[rows, cols].astype(f32), 0.0).astype(bf16)
            ones = jnp.where(keep, 1.0, 0.0).astype(bf16)
            values.append(jnp.concatenate([shown, ones], axis=1))
        for p in range(PMAX):
            keep = jnp.where(p < depth, 1.0, 0.0).astype(bf16)
            keys.append(pages[p][0, :, cols])
            ones = jnp.full((PAGE, LANES), 1.0, bf16) * keep
            values.append(jnp.concatenate([pages[p][1, :, cols] * keep, ones], axis=1))
        for b in range(blocks):
            rows = slice(b * PAGE, (b + 1) * PAGE)
            q = q_ref[rows, cols]
            ratios = []
            for side in range(2):
                q_side = jnp.where((lane // HD) == side, q, jnp.zeros_like(q))
                acc = jnp.zeros((PAGE, 2 * LANES), f32)
                for j in list(range(b + 1)) + list(range(blocks, blocks + PMAX)):
                    scores = lax.dot_general(
                        q_side, keys[j], (((1,), (1,)), ((), ())), preferred_element_type=f32
                    )
                    weights = jnp.exp(scores)
                    if j == b:
                        weights = jnp.where(causal, weights, 0.0)
                    acc += jnp.dot(weights.astype(bf16), values[j], preferred_element_type=f32)
                ratios.append(acc[:, :LANES] / acc[:, LANES:])
            out[rows, cols] = jnp.where((lane // HD) == 0, ratios[0], ratios[1]).astype(bf16)


def attend(live, depth, q, k, v, pages):
    tokens, width = q.shape
    heads = width // HD
    smem = pl.BlockSpec(memory_space=pltpu.SMEM)
    vmem = pl.BlockSpec(memory_space=pltpu.VMEM)
    keys = tokens + PMAX * PAGE
    return pl.pallas_call(
        attend_kernel,
        in_specs=[smem, smem] + [vmem] * 7,
        out_specs=vmem,
        out_shape=jax.ShapeDtypeStruct((tokens, width), bf16),
        compiler_params=params(),
        cost_estimate=cost(
            16 * heads * tokens * keys * HD, 2 * 1024 * 1024, heads * tokens * keys
        ),
        name="attend",
    )(live, depth, q, k, v, *pages)


def finish_kernel(slices, count, *refs):
    hidden, w_mine, w_theirs, rate = refs[:4]
    mine = refs[4 : 4 + count]
    theirs = refs[4 + count : 4 + 2 * count]
    out = refs[4 + 2 * count]

    def half(parts, weights):
        total = None
        for part, (start, size) in zip(parts, slices):
            term = jnp.dot(part[...], weights[start : start + size, :], preferred_element_type=f32)
            total = term if total is None else total + term
        return total

    branch = half(mine, w_mine) + half(theirs, w_theirs)
    hidden_f = hidden[...].astype(f32)
    anchor = hidden_f * lax.rsqrt(jnp.mean(hidden_f * hidden_f, axis=-1, keepdims=True) + epsilon)
    normed = branch * lax.rsqrt(jnp.mean(branch * branch, axis=-1, keepdims=True) + epsilon)
    updated = anchor + rate[...] * (normed - anchor)
    scale = lax.rsqrt(jnp.mean(updated * updated, axis=-1, keepdims=True) + epsilon)
    out[...] = (updated * scale).astype(bf16)


def finish(hidden_in, w_mine, w_theirs, rate, mine, theirs):
    tokens, depth = hidden_in.shape
    width = w_mine.shape[0]
    slices = group_slices(width)
    step = 256
    by_rows = lambda size: pl.BlockSpec((step, size), lambda i: (i, 0))
    whole = lambda shape: pl.BlockSpec(shape, lambda i: (0, 0))
    return pl.pallas_call(
        functools.partial(finish_kernel, slices, len(slices)),
        grid=(tokens // step,),
        in_specs=[by_rows(depth), whole(w_mine.shape), whole(w_theirs.shape), whole(rate.shape)]
        + [by_rows(size) for _, size in slices] * 2,
        out_specs=by_rows(depth),
        out_shape=jax.ShapeDtypeStruct((tokens, depth), bf16),
        compiler_params=params(),
        cost_estimate=cost(4 * tokens * depth * width, 8 * 1024 * 1024),
        name="finish",
    )(hidden_in, w_mine, w_theirs, rate, *mine, *theirs)


def body(
    hidden_in,
    w_query,
    w_key,
    w_value,
    w_out,
    head_gain,
    eigen_rate,
    pool_keys,
    pool_values,
    req_len,
    prefix_len,
    prefix_pages,
    placement,
):
    devices = lax.axis_size("blk")
    here = lax.axis_index("blk")
    kv_index = lax.axis_index("kv").astype(jnp.int32).reshape(1)
    blocks = hidden_in.shape[0] // PAGE
    gain = head_gain.reshape(1, -1)
    rate = eigen_rate.reshape(1, -1)

    page_offsets = [slot * devices // PMAX + 1 for slot in range(PMAX)]
    askers = (here - jnp.asarray(page_offsets, jnp.int32)) % devices
    local = prefix_pages[askers, jnp.arange(PMAX)] % pool_keys.shape[0]
    block_offsets = [(2 * b + 1) * devices // (2 * blocks) for b in range(blocks)]
    sources = (here - jnp.asarray(block_offsets, jnp.int32)) % devices
    slots = placement[sources * blocks + jnp.arange(blocks)] % blocks

    relay_send, page_send = pack(hidden_in, pool_keys, pool_values, local, kv_index, blocks)
    relay_mine = [from_behind(relay_send[b], "blk", block_offsets[b]) for b in range(blocks)]
    pages = [
        [from_behind(sent[s], "blk", devices - page_offsets[s]) for s in range(PMAX)]
        for sent in page_send
    ]
    w_theirs = from_behind(w_out, "kv", 1)
    projected = project(hidden_in, w_query, w_key, w_value, gain)
    relay_theirs = [from_behind(rows, "kv", 1) for rows in relay_mine]

    mine, theirs = [], []
    for g, (q, k, v) in enumerate(projected):
        attended = attend(req_len, prefix_len, q, k, v, pages[g])
        mine.append(attended)
        theirs.append(from_behind(attended, "kv", 1))
    new_keys, new_values = relay_project(
        relay_mine, relay_theirs, w_key, w_value, gain, kv_index, slots
    )
    layer_out = finish(hidden_in, w_out, w_theirs, rate, mine, theirs)
    return (layer_out, new_keys, new_values)


def solution(mesh):
    in_specs = (
        P("blk", None),
        P(None, "kv"),
        P(None, "kv"),
        P(None, "kv"),
        P("kv", None),
        P("kv"),
        P(),
        P("blk", None, "kv"),
        P("blk", None, "kv"),
        P("blk"),
        P("blk"),
        P(),
        P(),
    )
    out_specs = (P("blk", None), P("blk", None, "kv"), P("blk", None, "kv"))
    return jax.shard_map(body, mesh=mesh, in_specs=in_specs, out_specs=out_specs, check_vma=False)
```

time: 203 us -> 144 us (0.71)
  the two profiles are of different devices: /device:TPU:16 before, /device:TPU:0 now
where the time goes in v1:
time: 144 us; the launch traced here: 143 us
  Pallas kernels  46.6 us (32%)
  starting transfers between devices  44.2 us (31%)
  waiting for transfers between devices  26.3 us (18%)
  local copies, waits for them, and re-layouts  22.4 us (16%)
  between operations  2.22 us (2%)
    ppermute x20, starting transfers between devices, from_behind(): return lax.ppermute(block, axis, route)  44.2 us
    ppermute x20, waiting for transfers between devices, from_behind(): return lax.ppermute(block, axis, route)  26.3 us
    unnamed x88, local copies, waits for them, and re-layouts  19.9 us
    pallas_call x1, Pallas kernels, pack(): pl.pallas_call(functools.partial(pack_kernel, slices, blocks), grid_spec=...  18 us
    pallas_call x3, Pallas kernels, attend(): pl.pallas_call(attend_kernel, in_specs=[smem, smem] + [vmem] * 7, out_spe...  10.8 us
    pallas_call x1, Pallas kernels, project(): pl.pallas_call(functools.partial(project_kernel, slices), out_shape=outs,...  8.43 us
    pallas_call x1, Pallas kernels, relay_project(): pl.pallas_call(functools.partial(relay_kernel, group_slices(width), block...  5.09 us
    pallas_call x1, Pallas kernels, finish(): pl.pallas_call(functools.partial(finish_kernel, slices, len(slices)), gri...  4.29 us
  transfers between devices with their start and end apart: 20, of which 4 were waited for; matrix products, arithmetic and copies ran while one was open for 2% of the time, Pallas kernels for 17%

profile of v1, /device:TPU:0, one launch (start us, length us, event | category | flops | bytes accessed | tf_op | source)
XLA Modules:
  0.0 143.1 jit_solution(7371144855444657302)
XLA Ops:
  2.0 1.3 copy-done.1
  3.3 1.3 copy-done.4
  4.6 18.0 %pack.1 = (bf16[128,1280]{1,0:T(8,128)(2,1)S(1)}, bf16[128,1280]{1,0:T(8,128)(2,1)S(1)}, bf16[2,256,256]{2,1,0:T(8,128)(2,1)}, bf16[2,256,256]{2,1,0:T(8,128)(2,...) custom-call(s32[4]{0:T(128)S(1)} %and_select_fusion.2.local_ref, ...), custom_call_target="tpu_custom_call" | custom-call | tf_op jit(solution)/shard_map/pack/pallas_call | solution.py:80
  26.1 4.4 %collective-permute-start.10 = (bf16[2,256,128]{2,1,0:T(8,128)(2,1)S(1)}, bf16[2,256,128]{2,1,0:T(8,128)(2,1)S(1)}, u32[]{:S(2)}, u32[]{:S(2)}) collective-permute-start(bf16[2,256,128]{2,1,0:T(8,128)(2,1)S(1)} %get-tuple-element.46), channel_id=1, source_target_pairs={{5,0},{6,1},{7,2},{8,3},{9,4},{10,5},{11,6},{12,7},{13,8},{14,9},{... | collective-permute-start | bytes 393224 | tf_op jit(solution)/shard_map/ppermute | solution.py:27
  30.5 1.7 %collective-permute-start.5 = (bf16[2,256,256]{2,1,0:T(8,128)(2,1)S(1)}, bf16[2,256,256]{2,1,0:T(8,128)(2,1)S(1)}, u32[]{:S(2)}, u32[]{:S(2)}) collective-permute-start(bf16[2,256,256]{2,1,0:T(8,128)(2,1)S(1)} %get-tuple-element.38), channel_id=1, source_target_pairs={{1,0},{2,1},{3,2},{4,3},{5,4},{6,5},{7,6},{8,7},{9,8},{10,9},{11,1... | collective-permute-start | bytes 786440 | tf_op jit(solution)/shard_map/ppermute | solution.py:27
  32.3 2.6 %collective-permute-start.6 = (bf16[2,256,256]{2,1,0:T(8,128)(2,1)S(1)}, bf16[2,256,256]{2,1,0:T(8,128)(2,1)S(1)}, u32[]{:S(2)}, u32[]{:S(2)}) collective-permute-start(bf16[2,256,256]{2,1,0:T(8,128)(2,1)S(1)} %get-tuple-element.39), channel_id=1, source_target_pairs={{5,0},{6,1},{7,2},{8,3},{9,4},{10,5},{11,6},{12,7},{13,8},{14,9},{... | collective-permute-start | bytes 786440 | tf_op jit(solution)/shard_map/ppermute | solution.py:27
  34.8 1.5 %collective-permute-start = (bf16[640,1280]{1,0:T(8,128)(2,1)S(1)}, bf16[640,1280]{1,0:T(8,128)(2,1)S(1)}, u32[]{:S(2)}, u32[]{:S(2)}) collective-permute-start(bf16[640,1280]{1,0:T(8,128)(2,1)S(1)} %copy-done.3), channel_id=1, source_target_pairs={{16,0},{0,16},{17,1},{1,17},{18,2},{2,18},{19,3},{3,19},{20,4},{4,... | collective-permute-start | bytes 4915208 | tf_op jit(solution)/shard_map/ppermute | solution.py:27
  36.4 8.4 %project.1 = (bf16[512,256]{1,0:T(8,128)(2,1)S(1)}, bf16[512,256]{1,0:T(8,128)(2,1)S(1)}, bf16[512,256]{1,0:T(8,128)(2,1)S(1)}, bf16[512,256]{1,0:T(8,128)(2,1)S...) custom-call(bf16[512,1280]{1,0:T(8,128)(2,1)S(1)} %copy-done.1, ...), custom_call_target="tpu_custom_call" | custom-call | flops 2516582400 | bytes 8388608 | tf_op jit(solution)/shard_map/project/pallas_call | solution.py:147
  53.9 4.6 %collective-permute-start.1 = (bf16[2,256,256]{2,1,0:T(8,128)(2,1)}, bf16[2,256,256]{2,1,0:T(8,128)(2,1)}, u32[]{:S(2)}, u32[]{:S(2)}) collective-permute-start(bf16[2,256,256]{2,1,0:T(8,128)(2,1)} %get-tuple-element.31), channel_id=1, source_target_pairs={{1,0},{2,1},{3,2},{4,3},{5,4},{6,5},{7,6},{8,7},{9,8},{10,9},{11,1... | collective-permute-start | bytes 786440 | tf_op jit(solution)/shard_map/ppermute | solution.py:27
  59.2 1.2 gather_fusion.1
  60.4 7.7 %collective-permute-done.7.p2 = bf16[2,256,256]{2,1,0:T(8,128)(2,1)} collective-permute-done((bf16[2,256,256]{2,1,0:T(8,128)(2,1)}, bf16[2,256,256]{2,1,0:T(8,128)(2,1)}, u32[]{:S(2)}, u32[]{:S(2)}) %collective-permute-start.7) | collective-permute-done | bytes 262176 | tf_op jit(solution)/shard_map/ppermute | solution.py:27
  68.1 3.8 %collective-permute-start.17 = (bf16[128,1280]{1,0:T(8,128)(2,1)}, bf16[128,1280]{1,0:T(8,128)(2,1)S(1)}, u32[]{:S(2)}, u32[]{:S(2)}) collective-permute-start(bf16[128,1280]{1,0:T(8,128)(2,1)} %copy-done.8), channel_id=1, source_target_pairs={{4,0},{5,1},{6,2},{7,3},{8,4},{9,5},{10,6},{11,7},{12,8},{13,9},{1... | collective-permute-start | bytes 983048 | tf_op jit(solution)/shard_map/ppermute | solution.py:27
  74.6 3.4 %collective-permute-start.3 = (bf16[2,256,256]{2,1,0:T(8,128)(2,1)}, bf16[2,256,256]{2,1,0:T(8,128)(2,1)S(1)}, u32[]{:S(2)}, u32[]{:S(2)}) collective-permute-start(bf16[2,256,256]{2,1,0:T(8,128)(2,1)} %copy-done.10), channel_id=1, source_target_pairs={{9,0},{10,1},{11,2},{12,3},{13,4},{14,5},{15,6},{0,7},{1,8},{2,9},... | collective-permute-start | bytes 786440 | tf_op jit(solution)/shard_map/ppermute | solution.py:27
  78.0 7.1 %collective-permute-start.4 = (bf16[2,256,256]{2,1,0:T(8,128)(2,1)S(1)}, bf16[2,256,256]{2,1,0:T(8,128)(2,1)S(1)}, u32[]{:S(2)}, u32[]{:S(2)}) collective-permute-start(bf16[2,256,256]{2,1,0:T(8,128)(2,1)S(1)} %get-tuple-element.34), channel_id=1, source_target_pairs={{13,0},{14,1},{15,2},{0,3},{1,4},{2,5},{3,6},{4,7},{5,8},{6,9},{7,... | collective-permute-start | bytes 786440 | tf_op jit(solution)/shard_map/ppermute | solution.py:27
  89.9 4.5 %attend.4.refs_5_ = bf16[512,256]{1,0:T(8,128)(2,1)S(1)} custom-call(s32[1]{0:T(128)S(6)} %copy.18.live_ref, s32[1]{0:T(128)S(6)} %copy.19.depth_ref, bf16[512,256]{1,0:T(8,128)(2,1)S(1)} %copy-done.30, bf16[512,256]{1,0:T(8,128)(2,1)S(1)} %copy-done.32, bf16[512,256]{1,0:T(8,128)(2,1)S(1)} %copy-done.34, bf16[2,256,256]{2,1,0:T(8,128)(2,1)S(1)} %copy-done.12, ...), custom_call_target="tpu_custom_call" | custom-call | flops 3221225472 | bytes 2097152 | tf_op jit(solution)/shard_map/attend/pallas_call | solution.py:247
  94.4 7.7 %collective-permute-done.3.p2 = bf16[2,256,256]{2,1,0:T(8,128)(2,1)S(1)} collective-permute-done((bf16[2,256,256]{2,1,0:T(8,128)(2,1)}, bf16[2,256,256]{2,1,0:T(8,128)(2,1)S(1)}, u32[]{:S(2)}, u32[]{:S(2)}) %collective-permute-start.3) | collective-permute-done | bytes 262176 | tf_op jit(solution)/shard_map/ppermute | solution.py:27
  102.1 9.1 %collective-permute-start.9 = (bf16[2,256,128]{2,1,0:T(8,128)(2,1)S(1)}, bf16[2,256,128]{2,1,0:T(8,128)(2,1)S(1)}, u32[]{:S(2)}, u32[]{:S(2)}) collective-permute-start(bf16[2,256,128]{2,1,0:T(8,128)(2,1)S(1)} %copy-done.20), channel_id=1, source_target_pairs={{1,0},{2,1},{3,2},{4,3},{5,4},{6,5},{7,6},{8,7},{9,8},{10,9},{11,1... | collective-permute-start | bytes 393224 | tf_op jit(solution)/shard_map/ppermute | solution.py:27
  112.1 1.1 collective-permute-start.19
  113.3 4.5 %attend.3.refs_4_ = bf16[512,256]{1,0:T(8,128)(2,1)S(1)} custom-call(s32[1]{0:T(128)S(6)} %copy.18.live_ref, s32[1]{0:T(128)S(6)} %copy.19.depth_ref, bf16[512,256]{1,0:T(8,128)(2,1)S(1)} %copy-done.24, bf16[512,256]{1,0:T(8,128)(2,1)S(1)} %copy-done.26, bf16[512,256]{1,0:T(8,128)(2,1)S(1)} %copy-done.28, bf16[2,256,256]{2,1,0:T(8,128)(2,1)} %collective-permute-done.1.p0, ...), custom_call_target="tpu_custom_call" | custom-call | flops 3221225472 | bytes 2097152 | tf_op jit(solution)/shard_map/attend/pallas_call | solution.py:247
  119.9 1.9 %attend.5.refs_6_ = bf16[512,128]{1,0:T(8,128)(2,1)S(1)} custom-call(s32[1]{0:T(128)S(6)} %copy.18.live_ref, s32[1]{0:T(128)S(6)} %copy.19.depth_ref, bf16[512,128]{1,0:T(8,128)(2,1)S(1)} %copy-done.36, bf16[512,128]{1,0:T(8,128)(2,1)S(1)} %copy-done.38, bf16[512,128]{1,0:T(8,128)(2,1)S(1)} %copy-done.40, ...), custom_call_target="tpu_custom_call" | custom-call | flops 1610612736 | bytes 2097152 | tf_op jit(solution)/shard_map/attend/pallas_call | solution.py:247
  122.8 6.1 %collective-permute-done.19.refs_3_ = bf16[128,1280]{1,0:T(8,128)(2,1)S(1)} collective-permute-done((bf16[128,1280]{1,0:T(8,128)(2,1)S(1)}, bf16[128,1280]{1,0:T(8,128)(2,1)S(1)}, u32[]{:S(2)}, u32[]{:S(2)}) %collective-permute-start.19) | collective-permute-done | bytes 327712 | tf_op jit(solution)/shard_map/ppermute | solution.py:27
  128.9 5.1 %relay_project.1 = (bf16[2,256,640]{2,1,0:T(8,128)(2,1)}, bf16[2,256,640]{2,1,0:T(8,128)(2,1)}) custom-call(s32[1]{0:T(128)} %bitcast.2.kv_ref, s32[2]{0:T(128)S(1)} %and_select_fusion.slot_ref, bf16[128,1280]{1,0:T(8,128)(2,1)S(1)} %collective-permute-done.16.refs_0_, bf16[128,1280]{1,0:T(8,128)(2,1)S(1)} %collective-permute-done.17.refs_1_, ...), custom_call_target="tpu_custom_call" | custom-call | flops 1677721600 | bytes 8388608 | tf_op jit(solution)/shard_map/relay_project/pallas_call | solution.py:185
  134.0 4.8 %collective-permute-done.15.refs_9_ = bf16[512,128]{1,0:T(8,128)(2,1)S(1)} collective-permute-done((bf16[512,128]{1,0:T(8,128)(2,1)S(1)}, bf16[512,128]{1,0:T(8,128)(2,1)S(1)}, u32[]{:S(2)}, u32[]{:S(2)}) %collective-permute-start.15) | collective-permute-done | bytes 131104 | tf_op jit(solution)/shard_map/ppermute | solution.py:27
  138.8 4.3 %finish.1 = bf16[512,1280]{1,0:T(8,128)(2,1)} custom-call(bf16[512,1280]{1,0:T(8,128)(2,1)S(1)} %copy-done.2, bf16[640,1280]{1,0:T(8,128)(2,1)S(1)} %copy-done.3, bf16[640,1280]{1,0:T(8,128)(2,1)S(1)} %collective-permute-done.refs_2_, f32[1,1280]{1,0:T(1,128)S(1)} %reshape.15.refs_3_, bf16[512,256]{1,0:T(8,128)(2,1)S(1)} %attend.3.refs_4_, ...), custom_call_target="tpu_custom_call" | custom-call | flops 1677721600 | bytes 8388608 | tf_op jit(solution)/shard_map/finish/pallas_call | solution.py:289
  (120 shorter events, 24.9 us)
Async XLA Ops:
  4.6 30.2 %copy-start.3 = (bf16[640,1280]{1,0:T(8,128)(2,1)S(1)}, bf16[640,1280]{1,0:T(8,128)(2,1)}, u32[]{:S(2)}) copy-start(bf16[640,1280]{1,0:T(8,128)(2,1)} %refs_1_.1) | copy-start | bytes 4915204
  4.6 31.7 %copy-start.42 = (f32[640]{0:T(1024)S(1)}, f32[640]{0:T(1024)}, u32[]{:S(2)}) copy-start(f32[640]{0:T(1024)} %param.20) | copy-start | bytes 7684
  4.6 31.7 %copy-start.5 = (bf16[1280,640]{1,0:T(8,128)(2,1)S(1)}, bf16[1280,640]{1,0:T(8,128)(2,1)}, u32[]{:S(2)}) copy-start(bf16[1280,640]{1,0:T(8,128)(2,1)} %wq.1) | copy-start | bytes 4915204
  26.1 24.9 %collective-permute-start.10 = (bf16[2,256,128]{2,1,0:T(8,128)(2,1)S(1)}, bf16[2,256,128]{2,1,0:T(8,128)(2,1)S(1)}, u32[]{:S(2)}, u32[]{:S(2)}) collective-permute-start(bf16[2,256,128]{2,1,0:T(8,128)(2,1)S(1)} %get-tuple-element.46), channel_id=1, source_target_pairs={{5,0},{6,1},{7,2},{8,3},{9,4},{10,5},{11,6},{12,7},{13,8},{14,9},{... | collective-permute-start | bytes 393224 | tf_op jit(solution)/shard_map/ppermute | solution.py:27
  30.5 21.2 %collective-permute-start.11 = (bf16[2,256,128]{2,1,0:T(8,128)(2,1)S(1)}, bf16[2,256,128]{2,1,0:T(8,128)(2,1)S(1)}, u32[]{:S(2)}, u32[]{:S(2)}) collective-permute-start(bf16[2,256,128]{2,1,0:T(8,128)(2,1)S(1)} %get-tuple-element.47), channel_id=1, source_target_pairs={{9,0},{10,1},{11,2},{12,3},{13,4},{14,5},{15,6},{0,7},{1,8},{2,9},... | collective-permute-start | bytes 393224 | tf_op jit(solution)/shard_map/ppermute | solution.py:27
  30.5 22.7 %collective-permute-start.5 = (bf16[2,256,256]{2,1,0:T(8,128)(2,1)S(1)}, bf16[2,256,256]{2,1,0:T(8,128)(2,1)S(1)}, u32[]{:S(2)}, u32[]{:S(2)}) collective-permute-start(bf16[2,256,256]{2,1,0:T(8,128)(2,1)S(1)} %get-tuple-element.38), channel_id=1, source_target_pairs={{1,0},{2,1},{3,2},{4,3},{5,4},{6,5},{7,6},{8,7},{9,8},{10,9},{11,1... | collective-permute-start | bytes 786440 | tf_op jit(solution)/shard_map/ppermute | solution.py:27
  32.3 26.2 %collective-permute-start.6 = (bf16[2,256,256]{2,1,0:T(8,128)(2,1)S(1)}, bf16[2,256,256]{2,1,0:T(8,128)(2,1)S(1)}, u32[]{:S(2)}, u32[]{:S(2)}) collective-permute-start(bf16[2,256,256]{2,1,0:T(8,128)(2,1)S(1)} %get-tuple-element.39), channel_id=1, source_target_pairs={{5,0},{6,1},{7,2},{8,3},{9,4},{10,5},{11,6},{12,7},{13,8},{14,9},{... | collective-permute-start | bytes 786440 | tf_op jit(solution)/shard_map/ppermute | solution.py:27
  34.8 104.0 %collective-permute-start = (bf16[640,1280]{1,0:T(8,128)(2,1)S(1)}, bf16[640,1280]{1,0:T(8,128)(2,1)S(1)}, u32[]{:S(2)}, u32[]{:S(2)}) collective-permute-start(bf16[640,1280]{1,0:T(8,128)(2,1)S(1)} %copy-done.3), channel_id=1, source_target_pairs={{16,0},{0,16},{17,1},{1,17},{18,2},{2,18},{19,3},{3,19},{20,4},{4,... | collective-permute-start | bytes 4915208 | tf_op jit(solution)/shard_map/ppermute | solution.py:27
  51.7 16.4 %collective-permute-start.7 = (bf16[2,256,256]{2,1,0:T(8,128)(2,1)}, bf16[2,256,256]{2,1,0:T(8,128)(2,1)}, u32[]{:S(2)}, u32[]{:S(2)}) collective-permute-start(bf16[2,256,256]{2,1,0:T(8,128)(2,1)} %get-tuple-element.40), channel_id=1, source_target_pairs={{9,0},{10,1},{11,2},{12,3},{13,4},{14,5},{15,6},{0,7},{1,8},{2,9},... | collective-permute-start | bytes 786440 | tf_op jit(solution)/shard_map/ppermute | solution.py:27
  52.4 15.7 %collective-permute-start.8 = (bf16[2,256,256]{2,1,0:T(8,128)(2,1)}, bf16[2,256,256]{2,1,0:T(8,128)(2,1)}, u32[]{:S(2)}, u32[]{:S(2)}) collective-permute-start(bf16[2,256,256]{2,1,0:T(8,128)(2,1)} %get-tuple-element.41), channel_id=1, source_target_pairs={{13,0},{14,1},{15,2},{0,3},{1,4},{2,5},{3,6},{4,7},{5,8},{6,9},{7,... | collective-permute-start | bytes 786440 | tf_op jit(solution)/shard_map/ppermute | solution.py:27
  53.9 20.7 %collective-permute-start.1 = (bf16[2,256,256]{2,1,0:T(8,128)(2,1)}, bf16[2,256,256]{2,1,0:T(8,128)(2,1)}, u32[]{:S(2)}, u32[]{:S(2)}) collective-permute-start(bf16[2,256,256]{2,1,0:T(8,128)(2,1)} %get-tuple-element.31), channel_id=1, source_target_pairs={{1,0},{2,1},{3,2},{4,3},{5,4},{6,5},{7,6},{8,7},{9,8},{10,9},{11,1... | collective-permute-start | bytes 786440 | tf_op jit(solution)/shard_map/ppermute | solution.py:27
  59.2 18.8 %collective-permute-start.2 = (bf16[2,256,256]{2,1,0:T(8,128)(2,1)}, bf16[2,256,256]{2,1,0:T(8,128)(2,1)}, u32[]{:S(2)}, u32[]{:S(2)}) collective-permute-start(bf16[2,256,256]{2,1,0:T(8,128)(2,1)} %get-tuple-element.32), channel_id=1, source_target_pairs={{5,0},{6,1},{7,2},{8,3},{9,4},{10,5},{11,6},{12,7},{13,8},{14,9},{... | collective-permute-start | bytes 786440 | tf_op jit(solution)/shard_map/ppermute | solution.py:27
  68.1 43.1 %collective-permute-start.16 = (bf16[128,1280]{1,0:T(8,128)(2,1)}, bf16[128,1280]{1,0:T(8,128)(2,1)S(1)}, u32[]{:S(2)}, u32[]{:S(2)}) collective-permute-start(bf16[128,1280]{1,0:T(8,128)(2,1)} %copy-done.9), channel_id=1, source_target_pairs={{12,0},{13,1},{14,2},{15,3},{0,4},{1,5},{2,6},{3,7},{4,8},{5,9},{6... | collective-permute-start | bytes 983048 | tf_op jit(solution)/shard_map/ppermute | solution.py:27
  68.1 44.0 %collective-permute-start.17 = (bf16[128,1280]{1,0:T(8,128)(2,1)}, bf16[128,1280]{1,0:T(8,128)(2,1)S(1)}, u32[]{:S(2)}, u32[]{:S(2)}) collective-permute-start(bf16[128,1280]{1,0:T(8,128)(2,1)} %copy-done.8), channel_id=1, source_target_pairs={{4,0},{5,1},{6,2},{7,3},{8,4},{9,5},{10,6},{11,7},{12,8},{13,9},{1... | collective-permute-start | bytes 983048 | tf_op jit(solution)/shard_map/ppermute | solution.py:27
  74.6 27.5 %collective-permute-start.3 = (bf16[2,256,256]{2,1,0:T(8,128)(2,1)}, bf16[2,256,256]{2,1,0:T(8,128)(2,1)S(1)}, u32[]{:S(2)}, u32[]{:S(2)}) collective-permute-start(bf16[2,256,256]{2,1,0:T(8,128)(2,1)} %copy-done.10), channel_id=1, source_target_pairs={{9,0},{10,1},{11,2},{12,3},{13,4},{14,5},{15,6},{0,7},{1,8},{2,9},... | collective-permute-start | bytes 786440 | tf_op jit(solution)/shard_map/ppermute | solution.py:27
  78.0 24.1 %collective-permute-start.4 = (bf16[2,256,256]{2,1,0:T(8,128)(2,1)S(1)}, bf16[2,256,256]{2,1,0:T(8,128)(2,1)S(1)}, u32[]{:S(2)}, u32[]{:S(2)}) collective-permute-start(bf16[2,256,256]{2,1,0:T(8,128)(2,1)S(1)} %get-tuple-element.34), channel_id=1, source_target_pairs={{13,0},{14,1},{15,2},{0,3},{1,4},{2,5},{3,6},{4,7},{5,8},{6,9},{7,... | collective-permute-start | bytes 786440 | tf_op jit(solution)/shard_map/ppermute | solution.py:27
  89.9 23.4 %copy-start.26 = (bf16[512,256]{1,0:T(8,128)(2,1)S(1)}, bf16[512,256]{1,0:T(8,128)(2,1)}, u32[]{:S(2)}) copy-start(bf16[512,256]{1,0:T(8,128)(2,1)} %copy-done.25) | copy-start | bytes 786436
  102.1 15.7 %collective-permute-start.12 = (bf16[2,256,128]{2,1,0:T(8,128)(2,1)S(1)}, bf16[2,256,128]{2,1,0:T(8,128)(2,1)S(1)}, u32[]{:S(2)}, u32[]{:S(2)}) collective-permute-start(bf16[2,256,128]{2,1,0:T(8,128)(2,1)S(1)} %copy-done.22), channel_id=1, source_target_pairs={{13,0},{14,1},{15,2},{0,3},{1,4},{2,5},{3,6},{4,7},{5,8},{6,9},{7,... | collective-permute-start | bytes 393224 | tf_op jit(solution)/shard_map/ppermute | solution.py:27
  102.1 16.7 %collective-permute-start.9 = (bf16[2,256,128]{2,1,0:T(8,128)(2,1)S(1)}, bf16[2,256,128]{2,1,0:T(8,128)(2,1)S(1)}, u32[]{:S(2)}, u32[]{:S(2)}) collective-permute-start(bf16[2,256,128]{2,1,0:T(8,128)(2,1)S(1)} %copy-done.20), channel_id=1, source_target_pairs={{1,0},{2,1},{3,2},{4,3},{5,4},{6,5},{7,6},{8,7},{9,8},{10,9},{11,1... | collective-permute-start | bytes 393224 | tf_op jit(solution)/shard_map/ppermute | solution.py:27
  111.2 10.6 %collective-permute-start.18 = (bf16[128,1280]{1,0:T(8,128)(2,1)S(1)}, bf16[128,1280]{1,0:T(8,128)(2,1)S(1)}, u32[]{:S(2)}, u32[]{:S(2)}) collective-permute-start(bf16[128,1280]{1,0:T(8,128)(2,1)S(1)} %collective-permute-done.16.refs_0_), channel_id=1, source_target_pairs={{16,0},{0,16},{17,1},{1,17},{18,2},{2,18},{19,3},{3,19},{20,4},{4,... | collective-permute-start | bytes 983048 | tf_op jit(solution)/shard_map/ppermute | solution.py:27
  112.1 16.7 %collective-permute-start.19 = (bf16[128,1280]{1,0:T(8,128)(2,1)S(1)}, bf16[128,1280]{1,0:T(8,128)(2,1)S(1)}, u32[]{:S(2)}, u32[]{:S(2)}) collective-permute-start(bf16[128,1280]{1,0:T(8,128)(2,1)S(1)} %collective-permute-done.17.refs_1_), channel_id=1, source_target_pairs={{16,0},{0,16},{17,1},{1,17},{18,2},{2,18},{19,3},{3,19},{20,4},{4,... | collective-permute-start | bytes 983048 | tf_op jit(solution)/shard_map/ppermute | solution.py:27
  117.8 21.0 %collective-permute-start.14 = (bf16[512,256]{1,0:T(8,128)(2,1)S(1)}, bf16[512,256]{1,0:T(8,128)(2,1)S(1)}, u32[]{:S(2)}, u32[]{:S(2)}) collective-permute-start(bf16[512,256]{1,0:T(8,128)(2,1)S(1)} %attend.4.refs_5_), channel_id=1, source_target_pairs={{16,0},{0,16},{17,1},{1,17},{18,2},{2,18},{19,3},{3,19},{20,4},{4,... | collective-permute-start | bytes 786440 | tf_op jit(solution)/shard_map/ppermute | solution.py:27
  118.8 20.0 %collective-permute-start.13 = (bf16[512,256]{1,0:T(8,128)(2,1)S(1)}, bf16[512,256]{1,0:T(8,128)(2,1)S(1)}, u32[]{:S(2)}, u32[]{:S(2)}) collective-permute-start(bf16[512,256]{1,0:T(8,128)(2,1)S(1)} %attend.3.refs_4_), channel_id=1, source_target_pairs={{16,0},{0,16},{17,1},{1,17},{18,2},{2,18},{19,3},{3,19},{20,4},{4,... | collective-permute-start | bytes 786440 | tf_op jit(solution)/shard_map/ppermute | solution.py:27
  121.9 16.9 %collective-permute-start.15 = (bf16[512,128]{1,0:T(8,128)(2,1)S(1)}, bf16[512,128]{1,0:T(8,128)(2,1)S(1)}, u32[]{:S(2)}, u32[]{:S(2)}) collective-permute-start(bf16[512,128]{1,0:T(8,128)(2,1)S(1)} %attend.5.refs_6_), channel_id=1, source_target_pairs={{16,0},{0,16},{17,1},{1,17},{18,2},{2,18},{19,3},{3,19},{20,4},{4,... | collective-permute-start | bytes 393224 | tf_op jit(solution)/shard_map/ppermute | solution.py:27
  (40 other events, 199.4 us)
